TPU v7x, 32 devices: a whole 2x2x4 slice. The times are simulated.
32 devices in a mesh: groups: 1, expert: 16 (over z, y, x), tensor: 2 (over core).
Axes of the slice: x: 2, y: 2, z: 4, core: 2. Of those that a mesh axis runs over, the one named last changes fastest.
Arguments:
- tokens: bfloat16 [1024, 3584], P(('groups', 'expert'), 'tensor'), may hold values from -6 to 6
- expert_ids: int32 [1024, 8], P(('groups', 'expert')), may hold values from 0 to 15, all different within a row; in each aligned block of 64 rows (0 to 63, 64 to 127, ...) at most 36 rows name the same one
- route_weights: float32 [1024, 8], P(('groups', 'expert')), may hold values from 0.05 to 0.5
- gate_q: bfloat16 [16, 3584, 1024], P('expert', 'tensor'), may hold values from -4 to 4
- up_q: bfloat16 [16, 3584, 1024], P('expert', 'tensor'), may hold values from -4 to 4
- down_q: bfloat16 [16, 1024, 3584], P('expert', None, 'tensor'), may hold values from -4 to 4
- gate_scale: float32 [16, 28, 8], P('expert', 'tensor'), may hold values from 0.008351914 to 0.033407655
- up_scale: float32 [16, 28, 8], P('expert', 'tensor'), may hold values from 0.008351914 to 0.033407655
- down_scale: float32 [16, 8, 28], P('expert', None, 'tensor'), may hold values from 0.015625 to 0.0625
Outputs:
- mixed: bfloat16 [1024, 3584], P(('groups', 'expert'), 'tensor')
Inputs may be any that keep to these rules, and one draw needn't show every extreme that they name: `expert_ids`: within the 64 token rows of one index of expert, no expert is named by more than 36 rows, a bound that some block reaches; a row names 8 different experts.
All inputs are finite; a program needn't handle non-finite values.
Results may differ from a plain program's by a relative error of at most 0.0076.
Values may be sent and summed in bfloat16 or wider, within the bound.
A program may use at most 128 MiB of HBM per device.

v0:
```python
import jax
import jax.numpy as jnp
from jax import lax
from jax.sharding import PartitionSpec as P

FF = 1024


def dequant(quant, scales):
    height, breadth = quant.shape
    blocks = (
        quant.reshape(height // 128, 128, breadth // 128, 128).astype(jnp.float32)
        * scales[:, None, :, None]
    )
    return blocks.reshape(height, breadth).astype(jnp.bfloat16)


def local(
    tokens, expert_ids, route_weights, gate_q, up_q, down_q, gate_scale, up_scale, down_scale
):
    holders = lax.axis_size("expert")
    tok_rows, half_width = tokens.shape
    pick_count = expert_ids.shape[1]
    slices = FF // gate_q.shape[2]
    experts = holders // slices
    capacity = max(
        2, min(tok_rows, tok_rows * pick_count // experts + tok_rows * pick_count // (8 * experts))
    )
    slot_range = experts * capacity
    flat_ids = expert_ids.reshape(-1)
    onehot = (flat_ids[:, None] == jnp.arange(experts)[None, :]).astype(jnp.int32)
    before = jnp.cumsum(onehot, axis=0) - onehot
    position = jnp.sum(before * onehot, axis=1)
    slot_ids = flat_ids * capacity + position
    placing = (slot_ids[:, None] == jnp.arange(slot_range)[None, :]).astype(jnp.int32)
    pair_owner = jnp.arange(tok_rows * pick_count, dtype=jnp.int32) // pick_count
    token_of_slot = jnp.sum(placing * pair_owner[:, None], axis=0)
    occupied = jnp.sum(placing, axis=0) > 0
    filled = jnp.where(occupied[:, None], tokens[token_of_slot], jnp.zeros((), jnp.bfloat16))
    w_gate = dequant(gate_q[0], gate_scale[0])
    w_up = dequant(up_q[0], up_scale[0])
    w_down = dequant(down_q[0], down_scale[0])
    ff_width = w_gate.shape[1]
    outgoing = jnp.repeat(filled.reshape(experts, capacity, half_width), slices, axis=0)
    received = lax.all_to_all(outgoing, "expert", split_axis=0, concat_axis=0, tiled=True)
    sources, slots_here, _ = received.shape
    row_block = received.reshape(sources * slots_here, half_width)
    partial_value = jnp.concatenate(
        [
            jnp.dot(row_block, w_gate, preferred_element_type=jnp.float32),
            jnp.dot(row_block, w_up, preferred_element_type=jnp.float32),
        ],
        axis=1,
    )
    summed = lax.psum(partial_value, "tensor")
    hidden = (jax.nn.silu(summed[:, :ff_width]) * summed[:, ff_width:]).astype(jnp.bfloat16)
    term = jnp.dot(hidden, w_down, preferred_element_type=jnp.float32)
    result = term.astype(jnp.bfloat16).astype(jnp.float32)
    result = result.astype(jnp.bfloat16)
    returned = lax.all_to_all(
        result.reshape(sources, slots_here, half_width),
        "expert",
        split_axis=0,
        concat_axis=0,
        tiled=True,
    )
    combined = jnp.sum(
        returned.reshape(experts, slices, capacity, half_width).astype(jnp.float32), axis=1
    )
    rounded = lax.optimization_barrier(combined.astype(jnp.bfloat16)).astype(jnp.float32)
    flat_back = rounded.reshape(slot_range, half_width)
    picked = flat_back[slot_ids].reshape(tok_rows, pick_count, half_width)
    routed = jnp.zeros((tok_rows, half_width), jnp.float32)
    for column in range(pick_count):
        routed = routed + route_weights[:, column : column + 1] * picked[:, column]
    return routed.astype(jnp.bfloat16)


def solution(mesh):
    return jax.shard_map(
        local,
        mesh=mesh,
        in_specs=(
            P(("groups", "expert"), "tensor"),
            P(("groups", "expert"), None),
            P(("groups", "expert"), None),
            P("expert", "tensor", None),
            P("expert", "tensor", None),
            P("expert", None, "tensor"),
            P("expert", "tensor", None),
            P("expert", "tensor", None),
            P("expert", None, "tensor"),
        ),
        out_specs=P(("groups", "expert"), "tensor"),
        check_vma=False,
    )
```

profile of v0, /device:TPU:16, one launch (start us, length us, event | category | flops | bytes accessed | tf_op | source)
XLA Modules:
  0.0 218.2 jit_solution(18292867645373345725)
XLA Ops:
  6.5 0.8 copy.36
  7.5 1.2 reduce-window.6
  8.7 0.2 slice_reduce_fusion
  9.1 0.4 convert_reduce_fusion
  9.5 3.8 %gather_fusion = bf16[576,1792]{1,0:T(8,128)(2,1)} fusion(bf16[64,1792]{1,0:T(8,128)(2,1)S(1)} %copy-done, s32[1024]{0:T(1024)S(1)} %pad_clamp_fusion.1), kind=kCustom, calls=%fused_computation | custom fusion | bytes 4131072 | tf_op jit(solution)/shard_map/gather | solution.py:39
  13.3 2.5 %gather.9 = bf16[16,36,1792]{2,1,0:T(8,128)(2,1)S(1)} reshape(bf16[576,1792]{1,0:T(8,128)(2,1)} %gather_fusion) | data formatting | bytes 4128768 | tf_op jit(solution)/shard_map/gather | solution.py:39
  15.9 1.6 broadcast_select_fusion
  17.6 7.1 %all-to-all-start = ((bf16[16,36,1792]{2,1,0:T(8,128)(2,1)}), bf16[16,36,1792]{2,1,0:T(8,128)(2,1)S(1)}, u32[]{:S(2)}, u32[]{:S(2)}) async-start(bf16[16,36,1792]{2,1,0:T(8,128)(2,1)} %broadcast_select_fusion), calls=%async_computation | async-start | bytes 4587520 | tf_op jit(solution)/shard_map/all_to_all | solution.py:45
  24.7 2.9 %convert_bitcast_fusion = f32[224,8,8,128]{3,1,2,0:T(8,128)S(1)} fusion(bf16[1,1792,1024]{2,1,0:T(8,128)(2,1)} %param.13), kind=kLoop, calls=%fused_computation.8 | loop fusion | flops 1835008 | bytes 11010048
  27.7 4.8 %copy.63 = f32[224,8,8,128]{3,2,1,0:T(8,128)} copy(f32[224,8,8,128]{3,1,2,0:T(8,128)S(1)} %convert_bitcast_fusion) | data formatting | bytes 14680064
  32.5 2.9 %convert_bitcast_fusion.1 = f32[224,8,8,128]{3,1,2,0:T(8,128)S(1)} fusion(bf16[1,1792,1024]{2,1,0:T(8,128)(2,1)} %param.12), kind=kLoop, calls=%fused_computation.9 | loop fusion | flops 1835008 | bytes 11010048
  35.5 4.8 %copy.61 = f32[224,8,8,128]{3,2,1,0:T(8,128)} copy(f32[224,8,8,128]{3,1,2,0:T(8,128)S(1)} %convert_bitcast_fusion.1) | data formatting | bytes 14680064
  40.4 5.9 %fusion.1 = bf16[14,128,8,128]{3,2,1,0:T(8,128)(2,1)} fusion(f32[14,8]{1,0:T(8,128)S(1)} %copy.40, f32[14,128,8,128]{3,2,1,0:T(8,128)} %bitcast.152), kind=kLoop, calls=%fused_computation.5 | loop fusion | flops 3670016 | bytes 11010496 | tf_op jit(solution)/shard_map/convert_element_type | solution.py:15
  46.3 2.6 %fusion.2 = bf16[14,128,8,128]{3,2,1,0:T(8,128)(2,1)} fusion(f32[14,8]{1,0:T(8,128)S(1)} %copy.39, f32[14,128,8,128]{3,2,1,0:T(8,128)S(1)} %bitcast.153), kind=kLoop, calls=%fused_computation.7 | loop fusion | flops 3670016 | bytes 11010496 | tf_op jit(solution)/shard_map/convert_element_type | solution.py:15
  48.9 27.9 %all-to-all-done = bf16[16,36,1792]{2,1,0:T(8,128)(2,1)S(1)} async-done(((bf16[16,36,1792]{2,1,0:T(8,128)(2,1)}), bf16[16,36,1792]{2,1,0:T(8,128)(2,1)S(1)}, u32[]{:S(2)}, u32[]{:S(2)}) %all-to-all-start) | async-done | bytes 2064416 | tf_op jit(solution)/shard_map/all_to_all | solution.py:45
  76.8 2.0 reshape.158
  78.9 5.1 %fusion.5 = f32[576,1024]{1,0:T(8,128)S(1)} fusion(bf16[576,1792]{1,0:T(8,128)(2,1)} %reshape.158, bf16[224,8,8,128]{3,2,1,0:T(8,128)(2,1)} %bitcast.156), kind=kOutput, calls=%fused_computation.12 | convolution fusion | flops 2113929216 | bytes 8093696 | tf_op jit(solution)/shard_map/dot_general | solution.py:51
  84.0 2.3 %fusion.8 = f32[576,1024]{1,0:T(8,128)S(1)} fusion(bf16[576,1792]{1,0:T(8,128)(2,1)S(1)} %copy-done.5, bf16[224,8,8,128]{3,2,1,0:T(8,128)(2,1)S(1)} %bitcast.157), kind=kOutput, calls=%fused_computation.15 | convolution fusion | flops 2113929216 | bytes 8093696 | tf_op jit(solution)/shard_map/dot_general | solution.py:50
  86.3 2.5 %pad_maximum_fusion = f32[576,2048]{1,0:T(8,128)} fusion(f32[576,1024]{1,0:T(8,128)S(1)} %fusion.5, f32[576,1024]{1,0:T(8,128)S(1)} %fusion.8), kind=kLoop, calls=%fused_computation.10 | loop fusion | flops 1179648 | bytes 9437184 | tf_op jit(solution)/shard_map/concatenate | solution.py:48
  88.8 0.7 copy-done.9
  89.5 6.0 %copy.41 = bf16[1,1024,1792]{1,2,0:T(8,128)(2,1)} copy(bf16[1,1024,1792]{2,1,0:T(8,128)(2,1)} %param.14) | data formatting | bytes 7340032 | tf_op args[5]
  95.5 21.8 %all-reduce.2.cloned.1.call-done = f32[576,2048]{1,0:T(8,128)} async-done(((f32[576,2048]{1,0:T(8,128)}), f32[576,2048]{1,0:T(8,128)}) %all-reduce.2.cloned.1.call-update) | async-done | bytes 4718608 | tf_op jit(solution)/shard_map/psum | solution.py:55
  117.3 0.5 mul.186
  117.9 1.5 copy-done.3
  119.4 5.3 %fusion.12 = bf16[576,1792]{1,0:T(8,128)(2,1)S(1)} fusion(f32[224,8,8,128]{3,2,1,0:T(8,128)S(1)} %bitcast.155, bf16[1,1024,1792]{1,2,0:T(8,128)(2,1)S(1)} %copy-done.3, f32[576,2048]{1,0:T(8,128)} %all-reduce.2.cloned.1.call-done), kind=kOutput, calls=%fused_computation.19 | convolution fusion | flops 2124005376 | bytes 17793024 | tf_op jit(solution)/shard_map/dot_general | solution.py:57
  124.7 2.1 reshape.159
  126.8 7.0 %all-to-all-start.1 = ((bf16[16,36,1792]{2,1,0:T(8,128)(2,1)}), bf16[16,36,1792]{2,1,0:T(8,128)(2,1)S(1)}, u32[]{:S(2)}, u32[]{:S(2)}) async-start(bf16[16,36,1792]{2,1,0:T(8,128)(2,1)} %reshape.159), calls=%async_computation.1 | async-start | bytes 4587520 | tf_op jit(solution)/shard_map/all_to_all | solution.py:60
  134.0 52.4 %all-to-all-done.1 = bf16[16,36,1792]{2,1,0:T(8,128)(2,1)S(1)} async-done(((bf16[16,36,1792]{2,1,0:T(8,128)(2,1)}), bf16[16,36,1792]{2,1,0:T(8,128)(2,1)S(1)}, u32[]{:S(2)}, u32[]{:S(2)}) %all-to-all-start.1) | async-done | bytes 2064416 | tf_op jit(solution)/shard_map/all_to_all | solution.py:60
  186.4 2.5 %reshape.167 = f32[576,1792]{1,0:T(8,128)} reshape(bf16[16,36,1792]{2,1,0:T(8,128)(2,1)S(1)} %all-to-all-done.1) | data formatting | bytes 6193152 | tf_op jit(solution)/shard_map/reshape | solution.py:71
  188.9 7.1 %gather_fusion.1 = f32[512,1792]{1,0:T(8,128)} fusion(f32[576,1792]{1,0:T(8,128)} %reshape.167, s32[1024]{0:T(1024)S(1)} %pad_clamp_fusion), kind=kCustom, calls=%fused_computation.1 | custom fusion | bytes 7342080 | tf_op jit(solution)/shard_map/gather | solution.py:72
  196.0 14.3 %fusion.43 = (f32[64,1,1792]{2,1,0:T(1,128)S(1)}, f32[64,1,1792]{2,1,0:T(1,128)S(1)}, f32[64,1,1792]{2,1,0:T(1,128)S(1)}, f32[64,1,1792]{2,1,0:T(1,128)S(1)}, f3...) fusion(f32[64,8,1792]{2,1,0:T(8,128)} %bitcast.154), kind=kLoop, calls=%fused_computation.84 | loop fusion | bytes 7340032 | tf_op jit(solution)/shard_map/slice | solution.py:75
  210.3 1.0 fusion.20
  (42 shorter events, 1.0 us)
Async XLA Ops:
  6.5 3.0 %copy-start = (bf16[64,1792]{1,0:T(8,128)(2,1)S(1)}, bf16[64,1792]{1,0:T(8,128)(2,1)}, u32[]{:S(2)}) copy-start(bf16[64,1792]{1,0:T(8,128)(2,1)} %param.9) | copy-start | bytes 688132
  17.6 59.3 %all-to-all-start = ((bf16[16,36,1792]{2,1,0:T(8,128)(2,1)}), bf16[16,36,1792]{2,1,0:T(8,128)(2,1)S(1)}, u32[]{:S(2)}, u32[]{:S(2)}) async-start(bf16[16,36,1792]{2,1,0:T(8,128)(2,1)} %broadcast_select_fusion), calls=%async_computation | async-start | bytes 4587520 | tf_op jit(solution)/shard_map/all_to_all | solution.py:45
  24.7 92.7 %all-reduce.2.cloned.1.call-start = ((), (), s32[]{:S(2)}) async-start(), calls=%async_computation.2 | async-start | bytes 9437184 | tf_op jit(solution)/shard_map/psum | solution.py:55
  27.7 4.8 %copy-start.7 = (f32[1,14,8]{1,2,0:T(8,128)S(1)}, f32[1,14,8]{1,2,0:T(8,128)}, u32[]{:S(2)}) copy-start(f32[1,14,8]{1,2,0:T(8,128)} %param.16) | copy-start | bytes 1348
  35.5 4.9 %copy-start.8 = (f32[1,14,8]{1,2,0:T(8,128)S(1)}, f32[1,14,8]{1,2,0:T(8,128)}, u32[]{:S(2)}) copy-start(f32[1,14,8]{1,2,0:T(8,128)} %param.15) | copy-start | bytes 1348
  40.4 5.9 %copy-start.2 = (f32[224,8,8,128]{3,2,1,0:T(8,128)S(1)}, f32[224,8,8,128]{3,2,1,0:T(8,128)}, u32[]{:S(2)}) copy-start(f32[224,8,8,128]{3,2,1,0:T(8,128)} %copy.61) | copy-start | bytes 22020100
  78.9 5.1 %copy-start.4 = (bf16[14,128,8,128]{3,2,1,0:T(8,128)(2,1)S(1)}, bf16[14,128,8,128]{3,2,1,0:T(8,128)(2,1)}, u32[]{:S(2)}) copy-start(bf16[14,128,8,128]{3,2,1,0:T(8,128)(2,1)} %fusion.2) | copy-start | bytes 11010052
  78.9 5.1 %copy-start.5 = (bf16[576,1792]{1,0:T(8,128)(2,1)S(1)}, bf16[576,1792]{1,0:T(8,128)(2,1)}, u32[]{:S(2)}) copy-start(bf16[576,1792]{1,0:T(8,128)(2,1)} %reshape.158) | copy-start | bytes 6193156
  88.8 0.7 copy-start.9
  117.3 2.0 copy-start.3
  124.7 9.1 %copy-start.6 = (s32[64,8]{0,1:T(8,128)S(1)}, s32[64,8]{0,1:T(8,128)}, u32[]{:S(2)}) copy-start(s32[64,8]{0,1:T(8,128)} %param.10) | copy-start | bytes 6148
  124.7 9.3 %copy-start.10 = (f32[64,8]{0,1:T(8,128)S(1)}, f32[64,8]{0,1:T(8,128)}, u32[]{:S(2)}) copy-start(f32[64,8]{0,1:T(8,128)} %param.11) | copy-start | bytes 6148
  126.8 59.6 %all-to-all-start.1 = ((bf16[16,36,1792]{2,1,0:T(8,128)(2,1)}), bf16[16,36,1792]{2,1,0:T(8,128)(2,1)S(1)}, u32[]{:S(2)}, u32[]{:S(2)}) async-start(bf16[16,36,1792]{2,1,0:T(8,128)(2,1)} %reshape.159), calls=%async_computation.1 | async-start | bytes 4587520 | tf_op jit(solution)/shard_map/all_to_all | solution.py:60
  196.0 15.3 %copy-start.1 = (bf16[64,1792]{1,0:T(8,128)(2,1)S(1)}, bf16[64,1792]{1,0:T(8,128)(2,1)}, u32[]{:S(2)}) copy-start(bf16[64,1792]{1,0:T(8,128)(2,1)} %param.9) | copy-start | bytes 688132
Sparse Core Ops, SparseCore 0:
  88.9 28.3 all-reduce.1
where the time goes:
time: 219 us; the launch traced here: 218 us
  waiting for transfers between devices  102 us (47%)
  local copies, waits for them, and re-layouts  54.3 us (25%)
  other arithmetic  21.2 us (10%)
  starting transfers between devices  14.1 us (6%)
  between operations  13.6 us (6%)
  matrix products  12.7 us (6%)
    all_to_all x1, waiting for transfers between devices, local(): lax.all_to_all(result.reshape(sources, slots_here, half_width), 'expert',...  52.4 us
    all_to_all x1, waiting for transfers between devices, local(): lax.all_to_all(outgoing, 'expert', split_axis=0, concat_axis=0, tiled=True)  27.9 us
    psum x1, waiting for transfers between devices, local(): summed = lax.psum(partial_value, 'tensor')  21.8 us
    unnamed x26, local copies, waits for them, and re-layouts  18.6 us
    slice x1, local copies, waits for them, and re-layouts, local(): routed = routed + route_weights[:, column:column + 1] * picked[:, column]  14.3 us
    convert_element_type x2, other arithmetic, dequant(): return blocks.reshape(height, breadth).astype(jnp.bfloat16)  8.52 us
    all_to_all x1, starting transfers between devices, local(): lax.all_to_all(outgoing, 'expert', split_axis=0, concat_axis=0, tiled=True)  7.11 us
    gather x1, local copies, waits for them, and re-layouts, local(): picked = flat_back[slot_ids].reshape(tok_rows, pick_count, half_width)  7.09 us
  transfers between devices with their start and end apart: 3, of which 3 were waited for; matrix products, arithmetic and copies ran while one was open for 14% of the time, Pallas kernels for 0%

commit v1 on v0

--- a/solution.py
+++ b/solution.py
@@ -1,6 +1,8 @@
 import jax
 import jax.numpy as jnp
 from jax import lax
+from jax.experimental import pallas as pl
+from jax.experimental.pallas import tpu as pltpu
 from jax.sharding import PartitionSpec as P
 
 FF = 1024
@@ -15,7 +17,7 @@
     return blocks.reshape(height, breadth).astype(jnp.bfloat16)
 
 
-def local(
+def exchange_local(
     tokens, expert_ids, route_weights, gate_q, up_q, down_q, gate_scale, up_scale, down_scale
 ):
     holders = lax.axis_size("expert")
@@ -76,9 +78,307 @@
     return routed.astype(jnp.bfloat16)
 
 
+MESH = pl.DeviceIdType.MESH
+ROWS = 64
+
+
+def peer(e, d):
+    out = e
+    for bit in (1, 2, 4, 8):
+        if d & bit:
+            out = out + bit - 2 * bit * ((e // bit) % 2)
+    return out
+
+
+def fused_kernel(
+    tok_ref, ids_ref, rw_ref, gs_ref, us_ref, ds_ref, gate_hbm, up_hbm, down_hbm, out_ref,
+    tok, w_in, w_down, scale_in, scale_down, part_own, part_out, part_in, hid, part_y,
+    diag_in, near_in, far_in, col_out, z_in, wrow_out, wrow_in,
+    load_sem, tok_send, tok_recv, part_send, part_recv, row_send, row_recv,
+    y_send, y_recv, z_send, z_recv,
+):
+    e = lax.axis_index("expert")
+    c = lax.axis_index("tensor")
+    half = tok_ref.shape[1]
+    ff = w_down.shape[0]
+    loads = [
+        pltpu.make_async_copy(gate_hbm.at[0], w_in.at[0], load_sem.at[0]),
+        pltpu.make_async_copy(up_hbm.at[0], w_in.at[1], load_sem.at[1]),
+        pltpu.make_async_copy(down_hbm.at[0], w_down, load_sem.at[2]),
+    ]
+    for load in loads:
+        load.start()
+
+    barrier = pltpu.get_barrier_semaphore()
+    for d in range(1, 16):
+        pl.semaphore_signal(barrier, inc=1, device_id={"expert": peer(e, d)}, device_id_type=MESH)
+    pl.semaphore_signal(barrier, inc=1, device_id={"tensor": 1 - c}, device_id_type=MESH)
+
+    eye = lax.broadcasted_iota(jnp.int32, (ROWS, ROWS), 0) == lax.broadcasted_iota(
+        jnp.int32, (ROWS, ROWS), 1
+    )
+    ids = ids_ref[...]
+    rw = rw_ref[...]
+    for d in range(16):
+        column = jnp.sum(jnp.where(ids == peer(e, d), rw, 0.0), axis=1, keepdims=True)
+        row = jnp.sum(jnp.where(eye, column, 0.0), axis=0, keepdims=True)
+        wrow_out[d, :, 0:ROWS] = jnp.broadcast_to(row, (8, ROWS))
+    tok[0, 0] = tok_ref[...]
+    pl.semaphore_wait(barrier, 16)
+
+    def send(src, dst, s_sem, r_sem, **where):
+        return pltpu.make_async_remote_copy(
+            src_ref=src, dst_ref=dst, send_sem=s_sem, recv_sem=r_sem,
+            device_id=where, device_id_type=MESH,
+        )
+
+    tok_z = [
+        send(tok_ref, tok.at[0, dz], tok_send.at[0, dz], tok_recv.at[0, dz], expert=peer(e, 4 * dz))
+        for dz in range(1, 4)
+    ]
+    tok_xy = [
+        [
+            send(
+                tok.at[0, dz] if dz else tok_ref, tok.at[k, dz], tok_send.at[k, dz],
+                tok_recv.at[k, dz], expert=peer(e, k),
+            )
+            for k in (1, 2)
+        ]
+        for dz in range(4)
+    ]
+    near = 1 + c
+    far = 2 - c
+    near_dev = e + (1 - c) * (1 - 2 * (e % 2)) + c * (2 - 4 * ((e // 2) % 2))
+    far_dev = e + c * (1 - 2 * (e % 2)) + (1 - c) * (2 - 4 * ((e // 2) % 2))
+    tok_diag = [
+        send(tok.at[near, dz], tok.at[3, dz], tok_send.at[3, dz], tok_recv.at[3, dz], expert=far_dev)
+        for dz in range(4)
+    ]
+
+    def wait_tok(k, dz):
+        send(tok.at[k, dz], tok.at[k, dz], tok_send.at[0, 0], tok_recv.at[k, dz], expert=near_dev).wait_recv()
+
+    for cp in tok_xy[0]:
+        cp.start()
+    for cp in tok_z:
+        cp.start()
+    rows_sent = [
+        send(wrow_out.at[d], wrow_in.at[d], row_send.at[d], row_recv.at[d], expert=peer(e, d))
+        for d in range(1, 16)
+    ]
+    for cp in rows_sent:
+        cp.start()
+
+    wrow_in[0] = wrow_out[0]
+    for g, ref in ((0, gs_ref), (1, us_ref)):
+        blocks = ref[0]
+        for j in range(ff // 128):
+            scale_in[g, 0 : half // 128, j * 128 : (j + 1) * 128] = jnp.broadcast_to(
+                blocks[:, j : j + 1], (half // 128, 128)
+            )
+    blocks = ds_ref[0]
+    for j in range(half // 128):
+        scale_down[:, j * 128 : (j + 1) * 128] = jnp.broadcast_to(blocks[:, j : j + 1], (ff // 128, 128))
+
+    def dequant_in(g):
+        loads[g].wait()
+
+        @pl.loop(0, half // 128)
+        def _(i):
+            at = pl.ds(pl.multiple_of(i * 128, 128), 128)
+            w_in[g, at, :] = (w_in[g, at, :].astype(jnp.float32) * scale_in[g, pl.ds(i, 1), :]).astype(jnp.bfloat16)
+
+    def dequant_down():
+        loads[2].wait()
+
+        @pl.loop(0, ff // 128)
+        def _(i):
+            at = pl.ds(pl.multiple_of(i * 128, 128), 128)
+            w_down[at, :] = (w_down[at, :].astype(jnp.float32) * scale_down[pl.ds(i, 1), :]).astype(jnp.bfloat16)
+
+    def pass_on(dz):
+        tok_z[dz - 1].wait_recv()
+        for cp in tok_xy[dz]:
+            cp.start()
+
+    def pass_diag(dz):
+        wait_tok(near, dz)
+        tok_diag[dz].start()
+
+    parts = [
+        send(part_out.at[k], part_in.at[k], part_send.at[k], part_recv.at[k], tensor=1 - c)
+        for k in range(4)
+    ]
+
+    def gate_up(k):
+        x = tok[k].reshape(4 * ROWS, half)
+
+        @pl.loop(0, 2 * ff // 256)
+        def _(t):
+            g = t // (ff // 256)
+            at = pl.ds(pl.multiple_of((t % (ff // 256)) * 256, 256), 256)
+            p = jnp.dot(x, w_in[g, :, at], preferred_element_type=jnp.float32)
+            part_own[k % 2, g, :, at] = p
+            part_out[k, g, :, at] = p.astype(jnp.bfloat16)
+
+        parts[k].start()
+
+    def down(k):
+        parts[k].wait_recv()
+
+        @pl.loop(0, ff // 256)
+        def _(t):
+            at = pl.ds(pl.multiple_of(t * 256, 256), 256)
+            gate = part_own[k % 2, 0, :, at] + part_in[k, 0, :, at].astype(jnp.float32)
+            up = part_own[k % 2, 1, :, at] + part_in[k, 1, :, at].astype(jnp.float32)
+            hid[:, at] = (gate / (1.0 + jnp.exp(-gate)) * up).astype(jnp.bfloat16)
+
+        columns = []
+        for dz in range(4):
+            row = wrow_in[4 * dz + k, 0:1, 0:ROWS]
+            columns.append(jnp.sum(jnp.where(eye, row, 0.0), axis=1, keepdims=True))
+        column = jnp.concatenate(columns, axis=0)
+        h = hid[...]
+
+        @pl.loop(0, half // 256)
+        def _(t):
+            at = pl.ds(pl.multiple_of(t * 256, 256), 256)
+            y = jnp.dot(h, w_down[:, at], preferred_element_type=jnp.float32) * column
+            part_y[k, :, :, at] = y.reshape(4, ROWS, 256).astype(jnp.bfloat16)
+
+    diag_back = [
+        send(part_y.at[3, dz], diag_in.at[dz], y_send.at[0, dz], y_recv.at[0, dz], expert=near_dev)
+        for dz in range(4)
+    ]
+    near_back = [
+        send(part_y.at[near, dz], near_in.at[dz], y_send.at[1, dz], y_recv.at[1, dz], expert=near_dev)
+        for dz in range(4)
+    ]
+    far_back = [
+        send(part_y.at[far, dz], far_in.at[dz], y_send.at[2, dz], y_recv.at[2, dz], expert=far_dev)
+        for dz in range(4)
+    ]
+    z_back = [
+        send(col_out.at[dz], z_in.at[dz], z_send.at[dz], z_recv.at[dz], expert=peer(e, 4 * dz))
+        for dz in range(1, 4)
+    ]
+
+    dequant_in(0)
+    pass_diag(0)
+    pass_on(1)
+    dequant_in(1)
+    pass_on(2)
+    pass_diag(1)
+    dequant_down()
+    pass_on(3)
+    for cp in rows_sent:
+        cp.wait_recv()
+    gate_up(0)
+    pass_diag(2)
+    down(0)
+    pass_diag(3)
+    for dz in range(4):
+        wait_tok(far, dz)
+    gate_up(1)
+    gate_up(2)
+    down(1)
+    down(2)
+    for cp in near_back:
+        cp.start()
+    for dz in range(4):
+        tok_diag[dz].wait_recv()
+    gate_up(3)
+    down(3)
+    for cp in diag_back:
+        cp.start()
+    order = (1, 2, 3, 0)
+    for dz in order:
+        diag_back[dz].wait_recv()
+        part_y[far, dz] = (
+            part_y[far, dz].astype(jnp.float32) + diag_in[dz].astype(jnp.float32)
+        ).astype(jnp.bfloat16)
+        far_back[dz].start()
+    for dz in order:
+        near_back[dz].wait_recv()
+        far_back[dz].wait_recv()
+        total = (
+            part_y[0, dz].astype(jnp.float32)
+            + near_in[dz].astype(jnp.float32)
+            + far_in[dz].astype(jnp.float32)
+        )
+        if dz:
+            col_out[dz] = total.astype(jnp.bfloat16)
+            z_back[dz - 1].start()
+    for dz in range(1, 4):
+        z_back[dz - 1].wait_recv()
+        total = total + z_in[dz].astype(jnp.float32)
+    out_ref[...] = total.astype(jnp.bfloat16)
+
+    for cp in (
+        tok_z + rows_sent + parts + tok_diag + diag_back + near_back + far_back + z_back
+        + [cp for pair in tok_xy for cp in pair]
+    ):
+        cp.wait_send()
+
+
+def fused_local(
+    tokens, expert_ids, route_weights, gate_q, up_q, down_q, gate_scale, up_scale, down_scale
+):
+    rows, half = tokens.shape
+    ff = gate_q.shape[2]
+    bf16, f32 = jnp.bfloat16, jnp.float32
+    vmem = pl.BlockSpec(memory_space=pltpu.VMEM)
+    hbm = pl.BlockSpec(memory_space=pl.ANY)
+    dma = pltpu.SemaphoreType.DMA
+    return pl.pallas_call(
+        fused_kernel,
+        out_shape=jax.ShapeDtypeStruct((rows, half), bf16),
+        in_specs=[vmem] * 6 + [hbm] * 3,
+        out_specs=vmem,
+        scratch_shapes=[
+            pltpu.VMEM((4, 4, rows, half), bf16),
+            pltpu.VMEM((2, half, ff), bf16),
+            pltpu.VMEM((ff, half), bf16),
+            pltpu.VMEM((2, 16, ff), f32),
+            pltpu.VMEM((ff // 128, half), f32),
+            pltpu.VMEM((2, 2, 4 * rows, ff), f32),
+            pltpu.VMEM((4, 2, 4 * rows, ff), bf16),
+            pltpu.VMEM((4, 2, 4 * rows, ff), bf16),
+            pltpu.VMEM((4 * rows, ff), bf16),
+            pltpu.VMEM((4, 4, rows, half), bf16),
+            pltpu.VMEM((4, rows, half), bf16),
+            pltpu.VMEM((4, rows, half), bf16),
+            pltpu.VMEM((4, rows, half), bf16),
+            pltpu.VMEM((4, rows, half), bf16),
+            pltpu.VMEM((4, rows, half), bf16),
+            pltpu.VMEM((16, 8, 128), f32),
+            pltpu.VMEM((16, 8, 128), f32),
+            dma((3,)),
+            dma((4, 4)),
+            dma((4, 4)),
+            dma((4,)),
+            dma((4,)),
+            dma((16,)),
+            dma((16,)),
+            dma((3, 4)),
+            dma((3, 4)),
+            dma((4,)),
+            dma((4,)),
+        ],
+        compiler_params=pltpu.CompilerParams(
+            collective_id=0, has_side_effects=True, vmem_limit_bytes=58 * 1024 * 1024
+        ),
+        cost_estimate=pl.CostEstimate(
+            flops=2 * 16 * rows * half * ff * 3,
+            bytes_accessed=3 * 2 * half * ff,
+            transcendentals=16 * rows * ff,
+        ),
+    )(tokens, expert_ids, route_weights, gate_scale, up_scale, down_scale, gate_q, up_q, down_q)
+
+
 def solution(mesh):
     return jax.shard_map(
-        local,
+        fused_local if mesh.shape["expert"] == 16 and mesh.shape["tensor"] == 2 else exchange_local,
         mesh=mesh,
         in_specs=(
             P(("groups", "expert"), "tensor"),

time: 219 us -> 107 us (0.49)
  waiting for transfers between devices: 102 us -> 0 us
  Pallas kernels: 0 us -> 98.5 us
  local copies, waits for them, and re-layouts: 54.3 us -> 7.11 us
  other arithmetic: 21.2 us -> 0 us
  starting transfers between devices: 14.1 us -> 0 us
  between operations: 13.6 us -> 0.01 us
  matrix products: 12.7 us -> 0 us
    pallas_call x0 -> x1, Pallas kernels: none -> 98.5 us  [fused_local(): pl.pallas_call(fused_kernel, out_shape=jax.ShapeDtypeStruct((rows, half),...]
    all_to_all x2 -> x0, waiting for transfers between devices: 80.3 us -> none  [the longest x1 52.4 us: local(): lax.all_to_all(result.reshape(sources, slots_here, half_width), 'expert',...]
    psum x1 -> x0, waiting for transfers between devices: 21.8 us -> none  [local(): summed = lax.psum(partial_value, 'tensor')]
    slice x2 -> x0, local copies, waits for them, and re-layouts: 14.5 us -> none  [the longest x1 14.3 us: local(): routed = routed + route_weights[:, column:column + 1] * picked[:, column]]
    all_to_all x2 -> x0, starting transfers between devices: 14.1 us -> none  [the longest x1 7.11 us: local(): lax.all_to_all(outgoing, 'expert', split_axis=0, concat_axis=0, tiled=True)]
    gather x3 -> x0, local copies, waits for them, and re-layouts: 13.4 us -> none  [the longest x1 7.09 us: local(): picked = flat_back[slot_ids].reshape(tok_rows, pick_count, half_width)]
    dot_general x3 -> x0, matrix products: 12.7 us -> none  [the longest x1 5.33 us: local(): term = jnp.dot(hidden, w_down, preferred_element_type=jnp.float32)]
    unnamed x26 -> x5, local copies, waits for them, and re-layouts: 18.6 us -> 7.11 us
  transfers between devices with their start and end apart: 3 -> 0, of which waited for: 3 -> 0; matrix products, arithmetic and copies ran while one was open for 14% -> 0% of each run, Pallas kernels for 0% -> 0%
where the time goes in v1:
time: 107 us; the launch traced here: 106 us
  Pallas kernels  98.5 us (92%)
  local copies, waits for them, and re-layouts  7.11 us (7%)
    pallas_call x1, Pallas kernels, fused_local(): pl.pallas_call(fused_kernel, out_shape=jax.ShapeDtypeStruct((rows, half),...  98.5 us
    unnamed x5, local copies, waits for them, and re-layouts  7.11 us

profile of v1, /device:TPU:16, one launch (start us, length us, event | category | flops | bytes accessed | tf_op | source)
XLA Modules:
  0.0 105.6 jit_solution(3041565639880569528)
XLA Ops:
  0.0 1.4 %copy.12.gs_ref = f32[1,14,8]{2,1,0:T(8,128)} copy(f32[1,14,8]{1,2,0:T(8,128)} %param.15) | data formatting | bytes 896 | tf_op args[6]
  1.4 1.4 %copy.13.us_ref = f32[1,14,8]{2,1,0:T(8,128)} copy(f32[1,14,8]{1,2,0:T(8,128)} %param.16) | data formatting | bytes 896 | tf_op args[7]
  2.7 1.4 %copy.10.ids_ref = s32[64,8]{1,0:T(8,128)} copy(s32[64,8]{0,1:T(8,128)} %param.10) | data formatting | bytes 4096 | tf_op args[1]
  4.1 1.4 %copy.11.rw_ref = f32[64,8]{1,0:T(8,128)} copy(f32[64,8]{0,1:T(8,128)} %param.11) | data formatting | bytes 4096 | tf_op args[2]
  5.5 98.5 %shard_map.91 = bf16[64,1792]{1,0:T(8,128)(2,1)} custom-call(bf16[64,1792]{1,0:T(8,128)(2,1)} %tok_ref.1, s32[64,8]{1,0:T(8,128)} %copy.10.ids_ref, f32[64,8]{1,0:T(8,128)} %copy.11.rw_ref, f32[1,14,8]{2,1,0:T(8,128)} %copy.12.gs_ref, f32[1,14,8]{2,1,0:T(8,128)} %copy.13.us_ref, f32[1,8,14]{2,1,0:T(8,128)} %ds_ref.1, bf16[1,1792,1024]{2,1,0:T(8,128)(2,1)} %gate_hbm.1, ...), custom_call_target="tpu_custom_call" | custom-call | flops 11274289152 | bytes 11010048 | tf_op jit(solution)/shard_map/pallas_call | solution.py:333
  104.0 1.6 %copy.15 = bf16[64,1792]{1,0:T(8,128)(2,1)} copy(bf16[64,1792]{1,0:T(8,128)(2,1)} %shard_map.91) | data formatting | bytes 458752

commit v2 on v1

--- a/solution.py
+++ b/solution.py
@@ -93,7 +93,7 @@
 def fused_kernel(
     tok_ref, ids_ref, rw_ref, gs_ref, us_ref, ds_ref, gate_hbm, up_hbm, down_hbm, out_ref,
     tok, w_in, w_down, scale_in, scale_down, part_own, part_out, part_in, hid, part_y,
-    diag_in, near_in, far_in, col_out, z_in, wrow_out, wrow_in,
+    diag_in, near_in, far_in, col_out, z_in, acc, wrow_out, wrow_in,
     load_sem, tok_send, tok_recv, part_send, part_recv, row_send, row_recv,
     y_send, y_recv, z_send, z_recv,
 ):
@@ -120,8 +120,7 @@
     ids = ids_ref[...]
     rw = rw_ref[...]
     for d in range(16):
-        column = jnp.sum(jnp.where(ids == peer(e, d), rw, 0.0), axis=1, keepdims=True)
-        row = jnp.sum(jnp.where(eye, column, 0.0), axis=0, keepdims=True)
+        row = jnp.sum(jnp.where(ids == peer(e, d), rw, 0.0), axis=0, keepdims=True)
         wrow_out[d, :, 0:ROWS] = jnp.broadcast_to(row, (8, ROWS))
     tok[0, 0] = tok_ref[...]
     pl.semaphore_wait(barrier, 16)
@@ -133,14 +132,14 @@
         )
 
     tok_z = [
-        send(tok_ref, tok.at[0, dz], tok_send.at[0, dz], tok_recv.at[0, dz], expert=peer(e, 4 * dz))
+        send(tok_ref, tok.at[dz, 0], tok_send.at[dz, 0], tok_recv.at[dz, 0], expert=peer(e, 4 * dz))
         for dz in range(1, 4)
     ]
     tok_xy = [
         [
             send(
-                tok.at[0, dz] if dz else tok_ref, tok.at[k, dz], tok_send.at[k, dz],
-                tok_recv.at[k, dz], expert=peer(e, k),
+                tok.at[dz, 0] if dz else tok_ref, tok.at[dz, k], tok_send.at[dz, k],
+                tok_recv.at[dz, k], expert=peer(e, k),
             )
             for k in (1, 2)
         ]
@@ -151,12 +150,12 @@
     near_dev = e + (1 - c) * (1 - 2 * (e % 2)) + c * (2 - 4 * ((e // 2) % 2))
     far_dev = e + c * (1 - 2 * (e % 2)) + (1 - c) * (2 - 4 * ((e // 2) % 2))
     tok_diag = [
-        send(tok.at[near, dz], tok.at[3, dz], tok_send.at[3, dz], tok_recv.at[3, dz], expert=far_dev)
+        send(tok.at[dz, near], tok.at[dz, 3], tok_send.at[dz, 3], tok_recv.at[dz, 3], expert=far_dev)
         for dz in range(4)
     ]
 
     def wait_tok(k, dz):
-        send(tok.at[k, dz], tok.at[k, dz], tok_send.at[0, 0], tok_recv.at[k, dz], expert=near_dev).wait_recv()
+        send(tok.at[dz, k], tok.at[dz, k], tok_send.at[0, 0], tok_recv.at[dz, k], expert=near_dev).wait_recv()
 
     for cp in tok_xy[0]:
         cp.start()
@@ -170,11 +169,15 @@
         cp.start()
 
     wrow_in[0] = wrow_out[0]
+    square = (half // 128, half // 128)
+    diagonal = lax.broadcasted_iota(jnp.int32, square, 0) == lax.broadcasted_iota(jnp.int32, square, 1)
     for g, ref in ((0, gs_ref), (1, us_ref)):
         blocks = ref[0]
         for j in range(ff // 128):
+            row = blocks[j : j + 1, :]
+            column = jnp.sum(jnp.where(diagonal, row, 0.0), axis=1, keepdims=True)
             scale_in[g, 0 : half // 128, j * 128 : (j + 1) * 128] = jnp.broadcast_to(
-                blocks[:, j : j + 1], (half // 128, 128)
+                column, (half // 128, 128)
             )
     blocks = ds_ref[0]
     for j in range(half // 128):
@@ -211,6 +214,8 @@
     ]
 
     def gate_up(k):
+        wait_tok(far, k)
+        tok_diag[k].wait_recv()
         x = tok[k].reshape(4 * ROWS, half)
 
         @pl.loop(0, 2 * ff // 256)
@@ -234,8 +239,8 @@
             hid[:, at] = (gate / (1.0 + jnp.exp(-gate)) * up).astype(jnp.bfloat16)
 
         columns = []
-        for dz in range(4):
-            row = wrow_in[4 * dz + k, 0:1, 0:ROWS]
+        for d in range(4):
+            row = wrow_in[4 * k + d, 0:1, 0:ROWS]
             columns.append(jnp.sum(jnp.where(eye, row, 0.0), axis=1, keepdims=True))
         column = jnp.concatenate(columns, axis=0)
         h = hid[...]
@@ -247,15 +252,15 @@
             part_y[k, :, :, at] = y.reshape(4, ROWS, 256).astype(jnp.bfloat16)
 
     diag_back = [
-        send(part_y.at[3, dz], diag_in.at[dz], y_send.at[0, dz], y_recv.at[0, dz], expert=near_dev)
+        send(part_y.at[dz, 3], diag_in.at[dz], y_send.at[0, dz], y_recv.at[0, dz], expert=near_dev)
         for dz in range(4)
     ]
     near_back = [
-        send(part_y.at[near, dz], near_in.at[dz], y_send.at[1, dz], y_recv.at[1, dz], expert=near_dev)
+        send(part_y.at[dz, near], near_in.at[dz], y_send.at[1, dz], y_recv.at[1, dz], expert=near_dev)
         for dz in range(4)
     ]
     far_back = [
-        send(part_y.at[far, dz], far_in.at[dz], y_send.at[2, dz], y_recv.at[2, dz], expert=far_dev)
+        send(part_y.at[dz, far], far_in.at[dz], y_send.at[2, dz], y_recv.at[2, dz], expert=far_dev)
         for dz in range(4)
     ]
     z_back = [
@@ -263,56 +268,67 @@
         for dz in range(1, 4)
     ]
 
-    dequant_in(0)
-    pass_diag(0)
-    pass_on(1)
-    dequant_in(1)
-    pass_on(2)
-    pass_diag(1)
-    dequant_down()
-    pass_on(3)
-    for cp in rows_sent:
-        cp.wait_recv()
-    gate_up(0)
-    pass_diag(2)
-    down(0)
-    pass_diag(3)
-    for dz in range(4):
-        wait_tok(far, dz)
-    gate_up(1)
-    gate_up(2)
-    down(1)
-    down(2)
-    for cp in near_back:
-        cp.start()
-    for dz in range(4):
-        tok_diag[dz].wait_recv()
-    gate_up(3)
-    down(3)
-    for cp in diag_back:
-        cp.start()
-    order = (1, 2, 3, 0)
-    for dz in order:
+    def back(dz):
+        near_back[dz].start()
+        diag_back[dz].start()
+
+    def turn(dz):
         diag_back[dz].wait_recv()
-        part_y[far, dz] = (
-            part_y[far, dz].astype(jnp.float32) + diag_in[dz].astype(jnp.float32)
+        part_y[dz, far] = (
+            part_y[dz, far].astype(jnp.float32) + diag_in[dz].astype(jnp.float32)
         ).astype(jnp.bfloat16)
         far_back[dz].start()
-    for dz in order:
+
+    def column_sum(dz):
         near_back[dz].wait_recv()
         far_back[dz].wait_recv()
         total = (
-            part_y[0, dz].astype(jnp.float32)
+            part_y[dz, 0].astype(jnp.float32)
             + near_in[dz].astype(jnp.float32)
             + far_in[dz].astype(jnp.float32)
         )
         if dz:
             col_out[dz] = total.astype(jnp.bfloat16)
             z_back[dz - 1].start()
+        else:
+            acc[...] = total
+
+    dequant_in(0)
+    pass_diag(0)
+    pass_on(1)
+    dequant_in(1)
+    pass_on(2)
+    gate_up(0)
+    pass_diag(1)
+    dequant_down()
+    pass_on(3)
+    gate_up(1)
+    pass_diag(2)
+    for cp in rows_sent:
+        cp.wait_recv()
+    down(0)
+    back(0)
+    gate_up(2)
+    pass_diag(3)
+    turn(0)
+    down(1)
+    back(1)
+    gate_up(3)
+    turn(1)
+    down(2)
+    back(2)
+    column_sum(0)
+    down(3)
+    back(3)
+    column_sum(1)
+    turn(2)
+    turn(3)
+    column_sum(2)
+    column_sum(3)
     for dz in range(1, 4):
         z_back[dz - 1].wait_recv()
-        total = total + z_in[dz].astype(jnp.float32)
-    out_ref[...] = total.astype(jnp.bfloat16)
+        acc[...] += z_in[dz].astype(jnp.float32)
+    out_ref[...] = acc[...].astype(jnp.bfloat16)
 
     for cp in (
         tok_z + rows_sent + parts + tok_diag + diag_back + near_back + far_back + z_back
@@ -351,6 +367,7 @@
             pltpu.VMEM((4, rows, half), bf16),
             pltpu.VMEM((4, rows, half), bf16),
             pltpu.VMEM((4, rows, half), bf16),
+            pltpu.VMEM((rows, half), f32),
             pltpu.VMEM((16, 8, 128), f32),
             pltpu.VMEM((16, 8, 128), f32),
             dma((3,)),
@@ -373,7 +390,10 @@
             bytes_accessed=3 * 2 * half * ff,
             transcendentals=16 * rows * ff,
         ),
-    )(tokens, expert_ids, route_weights, gate_scale, up_scale, down_scale, gate_q, up_q, down_q)
+    )(
+        tokens, expert_ids.T, route_weights.T, gate_scale.swapaxes(1, 2), up_scale.swapaxes(1, 2),
+        down_scale, gate_q, up_q, down_q,
+    )
 
 
 def solution(mesh):

time: 107 us -> 98.1 us (0.917)
  local copies, waits for them, and re-layouts: 7.11 us -> 1.64 us
  Pallas kernels: 98.5 us -> 94.7 us
    unnamed x5 -> x1, local copies, waits for them, and re-layouts: 7.11 us -> 1.64 us
    pallas_call x1, Pallas kernels: 98.5 us -> 94.7 us  [fused_local(): pl.pallas_call(fused_kernel, out_shape=jax.ShapeDtypeStruct((rows, half),...]
where the time goes in v2:
time: 98.1 us; the launch traced here: 96.3 us
  Pallas kernels  94.7 us (97%)
  local copies, waits for them, and re-layouts  1.64 us (2%)
    pallas_call x1, Pallas kernels, fused_local(): pl.pallas_call(fused_kernel, out_shape=jax.ShapeDtypeStruct((rows, half),...  94.7 us

profile of v2, /device:TPU:16, one launch (start us, length us, event | category | flops | bytes accessed | tf_op | source)
XLA Modules:
  0.0 96.3 jit_solution(3368164699397660959)
XLA Ops:
  0.0 94.7 %shard_map.91 = bf16[64,1792]{1,0:T(8,128)(2,1)} custom-call(bf16[64,1792]{1,0:T(8,128)(2,1)} %tok_ref.1, s32[8,64]{1,0:T(8,128)} %bitcast.4, f32[8,64]{1,0:T(8,128)} %bitcast.5, f32[1,8,14]{2,1,0:T(8,128)} %bitcast.6, f32[1,8,14]{2,1,0:T(8,128)} %bitcast.7, f32[1,8,14]{2,1,0:T(8,128)} %ds_ref.1, bf16[1,1792,1024]{2,1,0:T(8,128)(2,1)} %gate_hbm.1, ...), custom_call_target="tpu_custom_call" | custom-call | flops 11274289152 | bytes 11010048 | tf_op jit(solution)/shard_map/pallas_call | solution.py:349
  94.7 1.6 %copy.11 = bf16[64,1792]{1,0:T(8,128)(2,1)} copy(bf16[64,1792]{1,0:T(8,128)(2,1)} %shard_map.91) | data formatting | bytes 458752

commit v3 on v2

--- a/solution.py
+++ b/solution.py
@@ -159,14 +159,12 @@
 
     for cp in tok_xy[0]:
         cp.start()
-    for cp in tok_z:
-        cp.start()
+    tok_z[0].start()
+    tok_z[1].start()
     rows_sent = [
         send(wrow_out.at[d], wrow_in.at[d], row_send.at[d], row_recv.at[d], expert=peer(e, d))
         for d in range(1, 16)
     ]
-    for cp in rows_sent:
-        cp.start()
 
     wrow_in[0] = wrow_out[0]
     square = (half // 128, half // 128)
@@ -201,6 +199,8 @@
 
     def pass_on(dz):
         tok_z[dz - 1].wait_recv()
+        if dz == 2:
+            tok_z[2].start()
         for cp in tok_xy[dz]:
             cp.start()
 
@@ -293,38 +293,40 @@
         else:
             acc[...] = total
 
-    dequant_in(0)
     pass_diag(0)
     pass_on(1)
+    for cp in rows_sent:
+        cp.start()
+    dequant_in(0)
     dequant_in(1)
     pass_on(2)
     gate_up(0)
     pass_diag(1)
     dequant_down()
-    pass_on(3)
-    gate_up(1)
-    pass_diag(2)
     for cp in rows_sent:
         cp.wait_recv()
     down(0)
     back(0)
-    gate_up(2)
-    pass_diag(3)
+    pass_diag(2)
+    gate_up(1)
     turn(0)
     down(1)
-    back(1)
-    gate_up(3)
-    turn(1)
+    gate_up(2)
+    pass_on(3)
     down(2)
     back(2)
+    pass_diag(3)
+    turn(2)
     column_sum(0)
+    gate_up(3)
+    column_sum(2)
     down(3)
     back(3)
+    back(1)
+    turn(3)
+    turn(1)
+    column_sum(3)
     column_sum(1)
-    turn(2)
-    turn(3)
-    column_sum(2)
-    column_sum(3)
     for dz in range(1, 4):
         z_back[dz - 1].wait_recv()
         acc[...] += z_in[dz].astype(jnp.float32)

time: 98.1 us -> 99.9 us (1.018)
  the two profiles are of different devices: /device:TPU:16 before, /device:TPU:0 now
where the time goes in v3:
time: 99.9 us; the launch traced here: 99.7 us
  Pallas kernels  98.1 us (98%)
  local copies, waits for them, and re-layouts  1.64 us (2%)
    pallas_call x1, Pallas kernels, fused_local(): pl.pallas_call(fused_kernel, out_shape=jax.ShapeDtypeStruct((rows, half),...  98.1 us

profile of v3, /device:TPU:0, one launch (start us, length us, event | category | flops | bytes accessed | tf_op | source)
XLA Modules:
  0.0 99.7 jit_solution(8446449120109668969)
XLA Ops:
  0.0 98.1 %shard_map.91 = bf16[64,1792]{1,0:T(8,128)(2,1)} custom-call(bf16[64,1792]{1,0:T(8,128)(2,1)} %tok_ref.1, s32[8,64]{1,0:T(8,128)} %bitcast.4, f32[8,64]{1,0:T(8,128)} %bitcast.5, f32[1,8,14]{2,1,0:T(8,128)} %bitcast.6, f32[1,8,14]{2,1,0:T(8,128)} %bitcast.7, f32[1,8,14]{2,1,0:T(8,128)} %ds_ref.1, bf16[1,1792,1024]{2,1,0:T(8,128)(2,1)} %gate_hbm.1, ...), custom_call_target="tpu_custom_call" | custom-call | flops 11274289152 | bytes 11010048 | tf_op jit(solution)/shard_map/pallas_call | solution.py:351
  98.1 1.6 %copy.11 = bf16[64,1792]{1,0:T(8,128)(2,1)} copy(bf16[64,1792]{1,0:T(8,128)(2,1)} %shard_map.91) | data formatting | bytes 458752

commit v4 on v2

--- a/solution.py
+++ b/solution.py
@@ -165,8 +165,6 @@
         send(wrow_out.at[d], wrow_in.at[d], row_send.at[d], row_recv.at[d], expert=peer(e, d))
         for d in range(1, 16)
     ]
-    for cp in rows_sent:
-        cp.start()
 
     wrow_in[0] = wrow_out[0]
     square = (half // 128, half // 128)
@@ -296,6 +294,8 @@
     dequant_in(0)
     pass_diag(0)
     pass_on(1)
+    for cp in rows_sent:
+        cp.start()
     dequant_in(1)
     pass_on(2)
     gate_up(0)
@@ -322,8 +322,8 @@
     back(3)
     column_sum(1)
     turn(2)
+    column_sum(2)
     turn(3)
-    column_sum(2)
     column_sum(3)
     for dz in range(1, 4):
         z_back[dz - 1].wait_recv()

time: 98.1 us -> 96.3 us (0.982); the launches traced: 96.3 us -> 96.1 us
  no operation moved by 1% of the time
where the time goes in v4:
time: 96.3 us; the launch traced here: 96.1 us
  Pallas kernels  94.5 us (98%)
  local copies, waits for them, and re-layouts  1.64 us (2%)
    pallas_call x1, Pallas kernels, fused_local(): pl.pallas_call(fused_kernel, out_shape=jax.ShapeDtypeStruct((rows, half),...  94.5 us

profile of v4, /device:TPU:16, one launch (start us, length us, event | category | flops | bytes accessed | tf_op | source)
XLA Modules:
  0.0 96.1 jit_solution(4433354714676247110)
XLA Ops:
  0.0 94.5 %shard_map.91 = bf16[64,1792]{1,0:T(8,128)(2,1)} custom-call(bf16[64,1792]{1,0:T(8,128)(2,1)} %tok_ref.1, s32[8,64]{1,0:T(8,128)} %bitcast.4, f32[8,64]{1,0:T(8,128)} %bitcast.5, f32[1,8,14]{2,1,0:T(8,128)} %bitcast.6, f32[1,8,14]{2,1,0:T(8,128)} %bitcast.7, f32[1,8,14]{2,1,0:T(8,128)} %ds_ref.1, bf16[1,1792,1024]{2,1,0:T(8,128)(2,1)} %gate_hbm.1, ...), custom_call_target="tpu_custom_call" | custom-call | flops 11274289152 | bytes 11010048 | tf_op jit(solution)/shard_map/pallas_call | solution.py:349
  94.5 1.6 %copy.11 = bf16[64,1792]{1,0:T(8,128)(2,1)} copy(bf16[64,1792]{1,0:T(8,128)(2,1)} %shard_map.91) | data formatting | bytes 458752

commit v5 on v4

--- a/solution.py
+++ b/solution.py
@@ -267,8 +267,8 @@
     ]
 
     def back(dz):
+        diag_back[dz].start()
         near_back[dz].start()
-        diag_back[dz].start()
 
     def turn(dz):
         diag_back[dz].wait_recv()

time: 96.3 us -> 91.6 us (0.951)
  Pallas kernels: 94.5 us -> 89.8 us
    pallas_call x1, Pallas kernels: 94.5 us -> 89.8 us  [fused_local(): pl.pallas_call(fused_kernel, out_shape=jax.ShapeDtypeStruct((rows, half),...]
where the time goes in v5:
time: 91.6 us; the launch traced here: 91.4 us
  Pallas kernels  89.8 us (98%)
  local copies, waits for them, and re-layouts  1.64 us (2%)
    pallas_call x1, Pallas kernels, fused_local(): pl.pallas_call(fused_kernel, out_shape=jax.ShapeDtypeStruct((rows, half),...  89.8 us

profile of v5, /device:TPU:16, one launch (start us, length us, event | category | flops | bytes accessed | tf_op | source)
XLA Modules:
  0.0 91.4 jit_solution(6070748426289266306)
XLA Ops:
  0.0 89.8 %shard_map.91 = bf16[64,1792]{1,0:T(8,128)(2,1)} custom-call(bf16[64,1792]{1,0:T(8,128)(2,1)} %tok_ref.1, s32[8,64]{1,0:T(8,128)} %bitcast.4, f32[8,64]{1,0:T(8,128)} %bitcast.5, f32[1,8,14]{2,1,0:T(8,128)} %bitcast.6, f32[1,8,14]{2,1,0:T(8,128)} %bitcast.7, f32[1,8,14]{2,1,0:T(8,128)} %ds_ref.1, bf16[1,1792,1024]{2,1,0:T(8,128)(2,1)} %gate_hbm.1, ...), custom_call_target="tpu_custom_call" | custom-call | flops 11274289152 | bytes 11010048 | tf_op jit(solution)/shard_map/pallas_call | solution.py:349
  89.8 1.6 %copy.11 = bf16[64,1792]{1,0:T(8,128)(2,1)} copy(bf16[64,1792]{1,0:T(8,128)(2,1)} %shard_map.91) | data formatting | bytes 458752
